TPU v7x, 32 devices: a whole 2x2x4 slice. The times are simulated.
32 devices in a mesh: gx: 8 (over y, x, core), gy: 4 (over z).
Axes of the slice: x: 2, y: 2, z: 4, core: 2. Of those that a mesh axis runs over, the one named last changes fastest.
Arguments:
- multipoles: float32 [10, 262144], P(None, ('gx', 'gy')), may hold values from -8 to 8
- fractions: float32 [3, 262144], P(None, ('gx', 'gy')), may hold values from 0 to 1
- base_index: int32 [3, 262144], P(None, ('gx', 'gy')), may hold values from 0 to 252, as said below
- block_plane: int32 [2048], P(('gx', 'gy')), may hold values from 0 to 7
- atom_count: int32 [2048], P(('gx', 'gy')), may hold values from 32 to 128, as said below
- coupling: float32 [8, 256, 256], replicated, may hold values from -0.375 to 0.375
Outputs:
- coupled: float32 [2, 256, 512, 256], P(None, ('gx', 'gy'))
Inputs may be any that keep to these rules, and one draw needn't show every extreme that they name: `base_index`: row 0 is an atom's x cell within its block's plane block, 0 to 7; row 1 its y cell within its device's 128 columns, 0 to 127; row 2 its z cell, 0 to 252. Atoms of the slots of device d lie in device d's cells. `atom_count`: slots of a block at or past its count are padding whose values are to be ignored.
All inputs are finite; a program needn't handle non-finite values.
Results may differ from a plain program's by a relative error of at most 0.0042.
Values sent between devices are 32-bit elements; how exact they have to be, the bound alone decides.
A program may use at most 128 MiB of HBM per device.

v0:
```python
import math

import jax
import jax.numpy as jnp
from jax import lax
from jax.sharding import PartitionSpec as P

NX = 512
NY = 512
NZ = 256
XB = 8
SLOT_BLK = 128
MBLK = 8
KX = 256


def from_behind(value, axis, by):
    devices = lax.axis_size(axis)
    return lax.ppermute(value, axis, [(i, (i + by) % devices) for i in range(devices)])


def spline_weights(fraction):
    remain = 1.0 - fraction
    square = fraction * fraction
    cubed = square * fraction
    values = jnp.stack(
        [
            remain * remain * remain / 6.0,
            (3.0 * cubed - 6.0 * square + 4.0) / 6.0,
            (-3.0 * cubed + 3.0 * square + 3.0 * fraction + 1.0) / 6.0,
            cubed / 6.0,
        ]
    )
    slopes = jnp.stack(
        [
            -remain * remain / 2.0,
            (3.0 * square - 4.0 * fraction) / 2.0,
            (-3.0 * square + 2.0 * fraction + 1.0) / 2.0,
            square / 2.0,
        ]
    )
    curves = jnp.stack([remain, 3.0 * fraction - 2.0, 1.0 - 3.0 * fraction, fraction])
    return jnp.stack([values, slopes, curves])


def plane_weights(moments, spline_x, spline_y):
    x_spline = spline_x[:, :, None]
    y_spline = spline_y[:, None, :]
    moment = moments[:, None, None]
    order_zero = (
        moment[0] * x_spline[0] * y_spline[0]
        + moment[1] * x_spline[1] * y_spline[0]
        + moment[2] * x_spline[0] * y_spline[1]
        + moment[4] * x_spline[2] * y_spline[0]
        + moment[5] * x_spline[0] * y_spline[2]
        + moment[7] * x_spline[1] * y_spline[1]
    )
    order_one = (
        moment[3] * x_spline[0] * y_spline[0]
        + moment[8] * x_spline[1] * y_spline[0]
        + moment[9] * x_spline[0] * y_spline[1]
    )
    order_two = moment[6] * x_spline[0] * y_spline[0]
    return jnp.stack([order_zero, order_one, order_two]).astype(jnp.bfloat16)


def selector(positions, width, tap_ids):
    window_ids = jnp.arange(width, dtype=jnp.int32)
    hits = window_ids[None, :, None, None] == positions[None, None] + tap_ids[:, None, None, None]
    return hits.astype(jnp.bfloat16)


def per_device(multipoles, fractions, base_index, block_plane, atom_count, coupling):
    cells_x = NX // lax.axis_size("gx")
    cells_y = NY // lax.axis_size("gy")
    block_count = block_plane.shape[0]
    slot_rank = jnp.arange(SLOT_BLK, dtype=jnp.int32)
    live_slot = (slot_rank[None, :] < atom_count[:, None]).astype(jnp.float32)
    moments = multipoles.reshape(10, block_count, SLOT_BLK) * live_slot[None]
    fraction = fractions.reshape(3, block_count, SLOT_BLK)
    cell_rows = base_index.reshape(3, block_count, SLOT_BLK)
    planes = plane_weights(moments, spline_weights(fraction[0]), spline_weights(fraction[1]))
    z_weights = spline_weights(fraction[2]).astype(jnp.bfloat16)
    width_x = XB + 3
    width_y = cells_y + 3
    tap_ids = jnp.arange(4, dtype=jnp.int32)
    per_turn = 4

    def spread_turn(turn, extended):
        first_block = turn * per_turn
        plane_part = lax.dynamic_slice_in_dim(planes, first_block, per_turn, 3)
        zweight_part = lax.dynamic_slice_in_dim(z_weights, first_block, per_turn, 2)
        cell_part = lax.dynamic_slice_in_dim(cell_rows, first_block, per_turn, 1)
        x_select = selector(cell_part[0], width_x, tap_ids)
        y_select = selector(cell_part[1], width_y, tap_ids)
        z_select = selector(cell_part[2], NZ, tap_ids)
        rows_y = jnp.einsum(
            "kabgs,bygs->kaygs", plane_part, y_select, preferred_element_type=jnp.float32
        ).astype(jnp.bfloat16)
        window = jnp.einsum(
            "axgs,kaygs->gkxys", x_select, rows_y, preferred_element_type=jnp.float32
        ).astype(jnp.bfloat16)
        z_window = jnp.einsum(
            "kcgs,czgs->gksz", zweight_part, z_select, preferred_element_type=jnp.float32
        ).astype(jnp.bfloat16)
        pieces = jnp.einsum(
            "gkxys,gksz->gxyz", window, z_window, preferred_element_type=jnp.float32
        )
        for member in range(per_turn):
            plane_start = block_plane[first_block + member] * XB
            current = lax.dynamic_slice(extended, (plane_start, 0, 0), (width_x, width_y, NZ))
            extended = lax.dynamic_update_slice(
                extended, current + pieces[member], (plane_start, 0, 0)
            )
        return extended

    extended = lax.fori_loop(
        0, block_count // per_turn, spread_turn, jnp.zeros((cells_x + 3, width_y, NZ), jnp.float32)
    )
    rim_x = from_behind(extended[cells_x:], "gx", 1)
    density = extended[:cells_x].at[:3].add(rim_x)
    rim_y = from_behind(density[:, cells_y:], "gy", 1)
    density = density[:, :cells_y].at[:, :3].add(rim_y)
    wave_x = jnp.arange(KX, dtype=jnp.int32)[:, None]
    cell_x = jnp.arange(NX, dtype=jnp.int32)[None, :]
    phase_x = (wave_x * cell_x % NX).astype(jnp.float32) * (2.0 * math.pi / NX)
    scale = 1.0 / math.sqrt(NX * NY)
    table_x = jnp.concatenate([jnp.cos(phase_x) * scale, -jnp.sin(phase_x) * scale], 0)
    lines = lax.all_to_all(density, "gx", split_axis=1, concat_axis=0, tiled=True)
    result = jnp.einsum("kx,xyz->kyz", table_x, lines, precision=lax.Precision.HIGHEST)
    spectrum = result.reshape(2, KX, lines.shape[1], lines.shape[2])
    spectrum = lax.all_to_all(
        lax.all_to_all(spectrum, "gx", split_axis=1, concat_axis=2, tiled=True),
        "gy",
        split_axis=1,
        concat_axis=2,
        tiled=True,
    )
    y_order = jnp.arange(NY, dtype=jnp.int32)
    wave_y = jnp.arange(NY, dtype=jnp.int32)[:, None]
    phase_y = (wave_y * y_order[None, :] % NY).astype(jnp.float32) * (2.0 * math.pi / NY)
    cosine_part = jnp.einsum(
        "qr,ckrz->ckqz", jnp.cos(phase_y), spectrum, precision=lax.Precision.HIGHEST
    )
    sine_part = jnp.einsum(
        "qr,ckrz->ckqz", jnp.sin(phase_y), spectrum, precision=lax.Precision.HIGHEST
    )
    real_part = cosine_part[0] + sine_part[1]
    imag_part = cosine_part[1] - sine_part[0]
    mode_rows = real_part.shape[0]
    stacked = jnp.stack([real_part, imag_part]).reshape(2, mode_rows, MBLK, NY // MBLK, NZ)
    coupled = jnp.einsum("ckbjw,bzw->ckbjz", stacked, coupling, precision=lax.Precision.HIGHEST)
    return coupled.reshape(2, mode_rows, NY, NZ)


def solution(mesh):
    return jax.shard_map(
        per_device,
        mesh=mesh,
        in_specs=(
            P(None, ("gx", "gy")),
            P(None, ("gx", "gy")),
            P(None, ("gx", "gy")),
            P(("gx", "gy")),
            P(("gx", "gy")),
            P(),
        ),
        out_specs=P(None, ("gx", "gy"), None, None),
        check_vma=False,
    )
```

profile of v0, /device:TPU:0, one launch (start us, length us, event | category | flops | bytes accessed | tf_op | source)
XLA Modules:
  0.0 1313.3 jit_solution(5332700107538207975)
XLA Ops:
  10.0 753.2 %while.19 = (s32[]{:T(128)}, f32[67,131,256]{2,1,0:T(8,128)}, s32[64]{0:T(128)S(1)}, s32[3,64,128]{2,1,0:T(8,128)S(1)}, bf16[3,4,4,64,128]{4,3,2,1,0:T(8,128)(2,...) while((s32[]{:T(128)}, f32[67,131,256]{2,1,0:T(8,128)}, ...), condition=%wide.region_1.0_spmd.clone.clone, body=%wide.region_0.0_spmd.clone.clone.sunk | while | flops 1166248448 | bytes 35086972 | solution.py:117
  13.6 14.1 %convert_bitcast_fusion.2 = bf16[4,3,11,131,128]{3,2,1,4,0:T(8,128)(2,1)} fusion(bf16[3,4,4,4,128]{2,1,0,4,3:T(4,128)(2,1)} %copy.117, s32[4,4,128]{0,2,1:T(8,128)S(1)} %iota_add_fusion.5, s32[4,4,128]{0,2,1:T(8,128)S(1)} %get-tuple-element.396), kind=kOutput, calls=%fused_computation.1.clone.1 | convolution fusion | flops 27454976 | bytes 4492288 | tf_op jit(solution)/shard_map/while/body/eval_jaxpr/axgs,kaygs->gkxys/dot_general | solution.py:100
  60.6 14.1 %convert_bitcast_fusion.2 = bf16[4,3,11,131,128]{3,2,1,4,0:T(8,128)(2,1)} fusion(bf16[3,4,4,4,128]{2,1,0,4,3:T(4,128)(2,1)} %copy.117, s32[4,4,128]{0,2,1:T(8,128)S(1)} %iota_add_fusion.5, s32[4,4,128]{0,2,1:T(8,128)S(1)} %get-tuple-element.396), kind=kOutput, calls=%fused_computation.1.clone.1 | convolution fusion | flops 27454976 | bytes 4492288 | tf_op jit(solution)/shard_map/while/body/eval_jaxpr/axgs,kaygs->gkxys/dot_general | solution.py:100
  107.7 14.1 %convert_bitcast_fusion.2 = bf16[4,3,11,131,128]{3,2,1,4,0:T(8,128)(2,1)} fusion(bf16[3,4,4,4,128]{2,1,0,4,3:T(4,128)(2,1)} %copy.117, s32[4,4,128]{0,2,1:T(8,128)S(1)} %iota_add_fusion.5, s32[4,4,128]{0,2,1:T(8,128)S(1)} %get-tuple-element.396), kind=kOutput, calls=%fused_computation.1.clone.1 | convolution fusion | flops 27454976 | bytes 4492288 | tf_op jit(solution)/shard_map/while/body/eval_jaxpr/axgs,kaygs->gkxys/dot_general | solution.py:100
  154.8 14.1 %convert_bitcast_fusion.2 = bf16[4,3,11,131,128]{3,2,1,4,0:T(8,128)(2,1)} fusion(bf16[3,4,4,4,128]{2,1,0,4,3:T(4,128)(2,1)} %copy.117, s32[4,4,128]{0,2,1:T(8,128)S(1)} %iota_add_fusion.5, s32[4,4,128]{0,2,1:T(8,128)S(1)} %get-tuple-element.396), kind=kOutput, calls=%fused_computation.1.clone.1 | convolution fusion | flops 27454976 | bytes 4492288 | tf_op jit(solution)/shard_map/while/body/eval_jaxpr/axgs,kaygs->gkxys/dot_general | solution.py:100
  201.9 14.1 %convert_bitcast_fusion.2 = bf16[4,3,11,131,128]{3,2,1,4,0:T(8,128)(2,1)} fusion(bf16[3,4,4,4,128]{2,1,0,4,3:T(4,128)(2,1)} %copy.117, s32[4,4,128]{0,2,1:T(8,128)S(1)} %iota_add_fusion.5, s32[4,4,128]{0,2,1:T(8,128)S(1)} %get-tuple-element.396), kind=kOutput, calls=%fused_computation.1.clone.1 | convolution fusion | flops 27454976 | bytes 4492288 | tf_op jit(solution)/shard_map/while/body/eval_jaxpr/axgs,kaygs->gkxys/dot_general | solution.py:100
  249.0 14.1 %convert_bitcast_fusion.2 = bf16[4,3,11,131,128]{3,2,1,4,0:T(8,128)(2,1)} fusion(bf16[3,4,4,4,128]{2,1,0,4,3:T(4,128)(2,1)} %copy.117, s32[4,4,128]{0,2,1:T(8,128)S(1)} %iota_add_fusion.5, s32[4,4,128]{0,2,1:T(8,128)S(1)} %get-tuple-element.396), kind=kOutput, calls=%fused_computation.1.clone.1 | convolution fusion | flops 27454976 | bytes 4492288 | tf_op jit(solution)/shard_map/while/body/eval_jaxpr/axgs,kaygs->gkxys/dot_general | solution.py:100
  296.0 14.1 %convert_bitcast_fusion.2 = bf16[4,3,11,131,128]{3,2,1,4,0:T(8,128)(2,1)} fusion(bf16[3,4,4,4,128]{2,1,0,4,3:T(4,128)(2,1)} %copy.117, s32[4,4,128]{0,2,1:T(8,128)S(1)} %iota_add_fusion.5, s32[4,4,128]{0,2,1:T(8,128)S(1)} %get-tuple-element.396), kind=kOutput, calls=%fused_computation.1.clone.1 | convolution fusion | flops 27454976 | bytes 4492288 | tf_op jit(solution)/shard_map/while/body/eval_jaxpr/axgs,kaygs->gkxys/dot_general | solution.py:100
  343.1 14.1 %convert_bitcast_fusion.2 = bf16[4,3,11,131,128]{3,2,1,4,0:T(8,128)(2,1)} fusion(bf16[3,4,4,4,128]{2,1,0,4,3:T(4,128)(2,1)} %copy.117, s32[4,4,128]{0,2,1:T(8,128)S(1)} %iota_add_fusion.5, s32[4,4,128]{0,2,1:T(8,128)S(1)} %get-tuple-element.396), kind=kOutput, calls=%fused_computation.1.clone.1 | convolution fusion | flops 27454976 | bytes 4492288 | tf_op jit(solution)/shard_map/while/body/eval_jaxpr/axgs,kaygs->gkxys/dot_general | solution.py:100
  390.2 14.2 %convert_bitcast_fusion.2 = bf16[4,3,11,131,128]{3,2,1,4,0:T(8,128)(2,1)} fusion(bf16[3,4,4,4,128]{2,1,0,4,3:T(4,128)(2,1)} %copy.117, s32[4,4,128]{0,2,1:T(8,128)S(1)} %iota_add_fusion.5, s32[4,4,128]{0,2,1:T(8,128)S(1)} %get-tuple-element.396), kind=kOutput, calls=%fused_computation.1.clone.1 | convolution fusion | flops 27454976 | bytes 4492288 | tf_op jit(solution)/shard_map/while/body/eval_jaxpr/axgs,kaygs->gkxys/dot_general | solution.py:100
  437.3 14.2 %convert_bitcast_fusion.2 = bf16[4,3,11,131,128]{3,2,1,4,0:T(8,128)(2,1)} fusion(bf16[3,4,4,4,128]{2,1,0,4,3:T(4,128)(2,1)} %copy.117, s32[4,4,128]{0,2,1:T(8,128)S(1)} %iota_add_fusion.5, s32[4,4,128]{0,2,1:T(8,128)S(1)} %get-tuple-element.396), kind=kOutput, calls=%fused_computation.1.clone.1 | convolution fusion | flops 27454976 | bytes 4492288 | tf_op jit(solution)/shard_map/while/body/eval_jaxpr/axgs,kaygs->gkxys/dot_general | solution.py:100
  484.5 14.1 %convert_bitcast_fusion.2 = bf16[4,3,11,131,128]{3,2,1,4,0:T(8,128)(2,1)} fusion(bf16[3,4,4,4,128]{2,1,0,4,3:T(4,128)(2,1)} %copy.117, s32[4,4,128]{0,2,1:T(8,128)S(1)} %iota_add_fusion.5, s32[4,4,128]{0,2,1:T(8,128)S(1)} %get-tuple-element.396), kind=kOutput, calls=%fused_computation.1.clone.1 | convolution fusion | flops 27454976 | bytes 4492288 | tf_op jit(solution)/shard_map/while/body/eval_jaxpr/axgs,kaygs->gkxys/dot_general | solution.py:100
  531.5 14.1 %convert_bitcast_fusion.2 = bf16[4,3,11,131,128]{3,2,1,4,0:T(8,128)(2,1)} fusion(bf16[3,4,4,4,128]{2,1,0,4,3:T(4,128)(2,1)} %copy.117, s32[4,4,128]{0,2,1:T(8,128)S(1)} %iota_add_fusion.5, s32[4,4,128]{0,2,1:T(8,128)S(1)} %get-tuple-element.396), kind=kOutput, calls=%fused_computation.1.clone.1 | convolution fusion | flops 27454976 | bytes 4492288 | tf_op jit(solution)/shard_map/while/body/eval_jaxpr/axgs,kaygs->gkxys/dot_general | solution.py:100
  578.6 14.1 %convert_bitcast_fusion.2 = bf16[4,3,11,131,128]{3,2,1,4,0:T(8,128)(2,1)} fusion(bf16[3,4,4,4,128]{2,1,0,4,3:T(4,128)(2,1)} %copy.117, s32[4,4,128]{0,2,1:T(8,128)S(1)} %iota_add_fusion.5, s32[4,4,128]{0,2,1:T(8,128)S(1)} %get-tuple-element.396), kind=kOutput, calls=%fused_computation.1.clone.1 | convolution fusion | flops 27454976 | bytes 4492288 | tf_op jit(solution)/shard_map/while/body/eval_jaxpr/axgs,kaygs->gkxys/dot_general | solution.py:100
  625.6 14.1 %convert_bitcast_fusion.2 = bf16[4,3,11,131,128]{3,2,1,4,0:T(8,128)(2,1)} fusion(bf16[3,4,4,4,128]{2,1,0,4,3:T(4,128)(2,1)} %copy.117, s32[4,4,128]{0,2,1:T(8,128)S(1)} %iota_add_fusion.5, s32[4,4,128]{0,2,1:T(8,128)S(1)} %get-tuple-element.396), kind=kOutput, calls=%fused_computation.1.clone.1 | convolution fusion | flops 27454976 | bytes 4492288 | tf_op jit(solution)/shard_map/while/body/eval_jaxpr/axgs,kaygs->gkxys/dot_general | solution.py:100
  672.6 14.1 %convert_bitcast_fusion.2 = bf16[4,3,11,131,128]{3,2,1,4,0:T(8,128)(2,1)} fusion(bf16[3,4,4,4,128]{2,1,0,4,3:T(4,128)(2,1)} %copy.117, s32[4,4,128]{0,2,1:T(8,128)S(1)} %iota_add_fusion.5, s32[4,4,128]{0,2,1:T(8,128)S(1)} %get-tuple-element.396), kind=kOutput, calls=%fused_computation.1.clone.1 | convolution fusion | flops 27454976 | bytes 4492288 | tf_op jit(solution)/shard_map/while/body/eval_jaxpr/axgs,kaygs->gkxys/dot_general | solution.py:100
  719.7 14.2 %convert_bitcast_fusion.2 = bf16[4,3,11,131,128]{3,2,1,4,0:T(8,128)(2,1)} fusion(bf16[3,4,4,4,128]{2,1,0,4,3:T(4,128)(2,1)} %copy.117, s32[4,4,128]{0,2,1:T(8,128)S(1)} %iota_add_fusion.5, s32[4,4,128]{0,2,1:T(8,128)S(1)} %get-tuple-element.396), kind=kOutput, calls=%fused_computation.1.clone.1 | convolution fusion | flops 27454976 | bytes 4492288 | tf_op jit(solution)/shard_map/while/body/eval_jaxpr/axgs,kaygs->gkxys/dot_general | solution.py:100
  805.6 91.9 %all-to-all-done = f32[64,128,256]{2,0,1:T(8,128)} async-done(((f32[64,128,256]{2,0,1:T(8,128)}), f32[64,128,256]{2,0,1:T(8,128)}, u32[]{:S(2)}, u32[]{:S(2)}) %all-to-all-start) | async-done | bytes 8388640 | tf_op jit(solution)/shard_map/all_to_all | solution.py:129
  901.5 14.5 %fusion.107 = f32[2,256,16,256]{3,1,2,0:T(8,128)S(1)} fusion(f32[2,256,512,1]{2,1,3,0:T(8,128)S(1)} %bitcast.183, f32[512,16,256,1]{2,0,1,3:T(8,128)S(1)} %bitcast.177), kind=kOutput, calls=%fused_computation.198 | convolution fusion | flops 12884901888 | bytes 17825792 | tf_op jit(solution)/shard_map/kx,xyz->kyz/dot_general | solution.py:130
  920.9 96.6 %all_to_all.54 = f32[2,256,16,256]{3,2,0,1:T(8,128)S(1)} all-to-all(f32[2,256,16,256]{3,2,0,1:T(8,128)S(1)} %copy.71), channel_id=1, replica_groups=mesh['gx'=8,'gy'=4] {'gx'}, dimensions={1} | all-to-all | bytes 16777216 | tf_op jit(solution)/shard_map/all_to_all | solution.py:133
  1019.9 186.6 %all_to_all.55 = f32[2,32,128,256]{3,2,0,1:T(8,128)} all-to-all(f32[2,32,128,256]{3,2,0,1:T(8,128)S(1)} %copy.74), channel_id=1, replica_groups=mesh['gx'=8,'gy'=4] {'gy'}, dimensions={1} | all-to-all | bytes 16777216 | tf_op jit(solution)/shard_map/all_to_all | solution.py:132
  1226.8 25.7 %convolution_bitcast_fusion = f32[2,8,512,256]{2,3,1,0:T(8,128)} fusion(f32[2,8,512,256]{2,3,1,0:T(8,128)} %all_to_all.50), kind=kOutput, calls=%fused_computation.48 | convolution fusion | flops 12888571904 | bytes 16777216 | tf_op jit(solution)/shard_map/qr,ckrz->ckqz/dot_general | solution.py:145
  1252.5 23.8 %convolution_bitcast_fusion.1 = f32[2,8,512,256]{2,3,1,0:T(8,128)} fusion(f32[2,8,512,256]{2,3,1,0:T(8,128)S(1)} %copy-done.1), kind=kOutput, calls=%fused_computation.49 | convolution fusion | flops 12888571904 | bytes 16777216 | tf_op jit(solution)/shard_map/qr,ckrz->ckqz/dot_general | solution.py:142
  1276.2 11.5 slice_add_fusion
  (277 shorter events, 593.7 us)
Async XLA Ops:
  0.0 1298.4 %copy-start = (f32[8,256,256]{2,1,0:T(8,128)S(1)}, f32[8,256,256]{2,1,0:T(8,128)}, u32[]{:S(2)}) copy-start(f32[8,256,256]{2,1,0:T(8,128)} %param.17) | copy-start | bytes 6291460
  4.3 5.7 copy-start.2
  764.3 12.0 collective-permute-start
  786.5 10.4 collective-permute-start.1
  798.5 99.0 %all-to-all-start = ((f32[64,128,256]{2,0,1:T(8,128)}), f32[64,128,256]{2,0,1:T(8,128)}, u32[]{:S(2)}, u32[]{:S(2)}) async-start(f32[64,128,256]{2,0,1:T(8,128)} %fusion.64), calls=%async_computation | async-start | bytes 16777216 | tf_op jit(solution)/shard_map/all_to_all | solution.py:129
  1226.8 25.7 %copy-start.1 = (f32[2,8,512,256]{2,3,1,0:T(8,128)S(1)}, f32[2,8,512,256]{2,3,1,0:T(8,128)}, u32[]{:S(2)}) copy-start(f32[2,8,512,256]{2,3,1,0:T(8,128)} %all_to_all.50) | copy-start | bytes 25165828
where the time goes:
time: 1330 us; the launch traced here: 1310 us
  matrix products  508 us (38%)
  blocking collectives  283 us (21%)
  other arithmetic  229 us (17%)
  local copies, waits for them, and re-layouts  150 us (11%)
  waiting for transfers between devices  91.9 us (7%)
  loops' own time  42.3 us (3%)
    dot_general x16, matrix products, spread_turn(): jnp.einsum('axgs,kaygs->gkxys', x_select, rows_y, preferred_element_type=...  226 us
    dynamic_update_slice x64, other arithmetic, spread_turn(): lax.dynamic_update_slice(extended, current + pieces[member], (plane_start...  205 us
    all_to_all x1, blocking collectives, per_device(): lax.all_to_all(lax.all_to_all(spectrum, 'gx', split_axis=1, concat_axis=2...  187 us
    dot_general x16, matrix products, spread_turn(): jnp.einsum('gkxys,gksz->gxyz', window, z_window, preferred_element_type=j...  181 us
    all_to_all x1, blocking collectives, per_device(): lax.all_to_all(spectrum, 'gx', split_axis=1, concat_axis=2, tiled=True)  96.6 us
    all_to_all x1, waiting for transfers between devices, per_device(): lax.all_to_all(density, 'gx', split_axis=1, concat_axis=0, tiled=True)  91.9 us
    dynamic_slice x32, local copies, waits for them, and re-layouts, spread_turn(): plane_part = lax.dynamic_slice_in_dim(planes, first_block, per_turn, 3)  50.7 us
    another operation x1, loops' own time, per_device(): lax.fori_loop(0, block_count // per_turn, spread_turn, jnp.zeros((cells_x...  42.3 us
  transfers between devices with their start and end apart: 3, of which 1 were waited for; matrix products, arithmetic and copies ran while one was open for 2% of the time, Pallas kernels for 0%

commit v1 on v0

v1 whole, which is shorter than its diff:
```python
import functools
import math

import jax
import jax.numpy as jnp
import numpy as np
from jax import lax
from jax.experimental import pallas as pl
from jax.experimental.pallas import tpu as pltpu
from jax.sharding import PartitionSpec as P

NX = 512
NY = 512
NZ = 256
XB = 8
SLOT_BLK = 128
MBLK = 8
KX = 256
GROUP = 8
PACK = 16


def from_behind(value, axis, by):
    devices = lax.axis_size(axis)
    return lax.ppermute(value, axis, [(i, (i + by) % devices) for i in range(devices)])


def spline_weights(u):
    r = 1.0 - u
    square = u * u
    cubed = square * u
    values = [
        r * r * r / 6.0,
        (3.0 * cubed - 6.0 * square + 4.0) / 6.0,
        (-3.0 * cubed + 3.0 * square + 3.0 * u + 1.0) / 6.0,
        cubed / 6.0,
    ]
    slopes = [
        -r * r / 2.0,
        (3.0 * square - 4.0 * u) / 2.0,
        (-3.0 * square + 2.0 * u + 1.0) / 2.0,
        square / 2.0,
    ]
    curves = [r, 3.0 * u - 2.0, 1.0 - 3.0 * u, u]
    return values, slopes, curves


def spread_kernel(
    plane_ref, count_ref, moment_ref, fraction_ref, cell_ref, out_ref, weight_ref, rows_ref
):
    step = pl.program_id(0)
    rows = out_ref.shape[1]
    padded = rows_ref.shape[1]
    bf16 = jnp.bfloat16

    @pl.when(step == 0)
    def _():
        def clear(plane, carry):
            out_ref[plane] = jnp.zeros((rows, NZ), jnp.float32)
            return carry

        lax.fori_loop(0, out_ref.shape[0], clear, 0)

    wx, dx, sx = spline_weights(fraction_ref[0])
    wy, dy, sy = spline_weights(fraction_ref[1])
    z_taps = spline_weights(fraction_ref[2])
    m = [moment_ref[i] for i in range(10)]
    for a in range(4):
        base = m[0] * wx[a] + m[1] * dx[a] + m[4] * sx[a]
        slope = m[2] * wx[a] + m[7] * dx[a]
        curve = m[5] * wx[a]
        one_base = m[3] * wx[a] + m[8] * dx[a]
        one_slope = m[9] * wx[a]
        two = m[6] * wx[a]
        for b in range(4):
            weight_ref[a * 4 + b] = base * wy[b] + slope * dy[b] + curve * sy[b]
            weight_ref[16 + a * 4 + b] = one_base * wy[b] + one_slope * dy[b]
            weight_ref[32 + a * 4 + b] = two * wy[b]
    for k in range(3):
        for c in range(4):
            weight_ref[48 + k * 4 + c] = z_taps[k][c]

    lane = lax.broadcasted_iota(jnp.int32, (1, SLOT_BLK), 1)

    def spans(tile, count):
        return jnp.concatenate([tile] * count, axis=0)

    def packed(row):
        return jnp.broadcast_to(row, (PACK, SLOT_BLK)).astype(bf16)

    y_count = padded // PACK
    z_count = NZ // PACK

    def one_block(g, carry):
        block = step * GROUP + g
        alive = lane < count_ref[block]
        x_cell = packed(cell_ref[0, pl.ds(g, 1), :].astype(jnp.float32))
        y_row = jnp.where(alive, cell_ref[1, pl.ds(g, 1), :], -1024).astype(jnp.float32)
        z_row = cell_ref[2, pl.ds(g, 1), :].astype(jnp.float32)

        def weight(index):
            return packed(weight_ref[index, pl.ds(g, 1), :])

        def chosen(hits, index, count):
            zero = jnp.zeros((count * PACK, SLOT_BLK), bf16)
            total = zero
            for tap in range(4):
                total = jnp.where(hits[tap], spans(weight(index + tap), count), total)
            return total

        y_ids = lax.broadcasted_iota(jnp.int32, (padded, SLOT_BLK), 0).astype(jnp.float32)
        y_ids = y_ids.astype(bf16)
        y_hits = [y_ids == spans(packed(y_row + float(b)), y_count) for b in range(4)]
        for k in range(3):
            for a in range(4):
                rows_ref[k * 4 + a] = chosen(y_hits, k * 16 + a * 4, y_count)
        z_ids = lax.broadcasted_iota(jnp.int32, (NZ, SLOT_BLK), 0).astype(jnp.float32)
        z_ids = z_ids.astype(bf16)
        z_hits = [z_ids == spans(packed(z_row + float(c)), z_count) for c in range(4)]
        z_window = jnp.concatenate(
            [chosen(z_hits, 48 + k * 4, z_count) for k in range(3)], axis=1
        )
        plane = plane_ref[block] * XB
        zero = jnp.zeros((padded, SLOT_BLK), bf16)
        for first, count in ((0, 4), (4, 4), (8, 3)):
            parts = []
            for x in range(first, first + count):
                pieces = []
                for k in range(3):
                    total = zero
                    for a in range(4):
                        if 0 <= x - a < XB:
                            hit = x_cell == jnp.full((PACK, SLOT_BLK), x - a, bf16)
                            total = jnp.where(spans(hit, y_count), rows_ref[k * 4 + a], total)
                    pieces.append(total)
                parts.append(jnp.concatenate(pieces, axis=1))
            window = jnp.concatenate(parts, axis=0)
            result = lax.dot_general(
                window, z_window, (((1,), (1,)), ((), ())), preferred_element_type=jnp.float32
            )
            for i in range(count):
                out_ref[plane + first + i] += result[i * padded : i * padded + rows]
        return carry

    lax.fori_loop(0, GROUP, one_block, 0)


def spread(multipoles, fractions, base_index, block_plane, atom_count, cells_x, cells_y):
    blocks = block_plane.shape[0]
    rows = -(-(cells_y + 3) // 8) * 8
    padded = -(-(cells_y + 3) // PACK) * PACK

    def part(height):
        return pl.BlockSpec((height, GROUP, SLOT_BLK), lambda i, *_: (0, i, 0))

    return pl.pallas_call(
        spread_kernel,
        out_shape=jax.ShapeDtypeStruct((cells_x + 3, rows, NZ), jnp.float32),
        grid_spec=pltpu.PrefetchScalarGridSpec(
            num_scalar_prefetch=2,
            grid=(blocks // GROUP,),
            in_specs=[part(10), part(3), part(3)],
            out_specs=pl.BlockSpec((cells_x + 3, rows, NZ), lambda i, *_: (0, 0, 0)),
            scratch_shapes=[
                pltpu.VMEM((60, GROUP, SLOT_BLK), jnp.float32),
                pltpu.VMEM((12, padded, SLOT_BLK), jnp.bfloat16),
            ],
        ),
        compiler_params=pltpu.CompilerParams(vmem_limit_bytes=48 * 1024 * 1024),
    )(
        block_plane,
        atom_count,
        multipoles.reshape(10, blocks, SLOT_BLK),
        fractions.reshape(3, blocks, SLOT_BLK),
        base_index.reshape(3, blocks, SLOT_BLK),
    )


def phases(waves, cells, size):
    return (np.arange(waves)[:, None] * np.arange(cells)[None, :] % size) * (2.0 * math.pi / size)


def per_device(multipoles, fractions, base_index, block_plane, atom_count, coupling):
    cells_x = NX // lax.axis_size("gx")
    cells_y = NY // lax.axis_size("gy")
    extended = spread(
        multipoles, fractions, base_index, block_plane, atom_count, cells_x, cells_y
    )
    rim_x = from_behind(extended[cells_x:, : cells_y + 3], "gx", 1)
    spill = extended[:cells_x, cells_y : cells_y + 3].at[:3].add(rim_x[:, cells_y:])
    rim_y = from_behind(spill, "gy", 1)
    density = (
        extended[:cells_x, :cells_y]
        + jnp.pad(rim_x[:, :cells_y], ((0, cells_x - 3), (0, 0), (0, 0)))
        + jnp.pad(rim_y, ((0, 0), (0, cells_y - 3), (0, 0)))
    )
    phase_x = phases(KX, NX, NX)
    scale = 1.0 / math.sqrt(NX * NY)
    table_x = np.concatenate([np.cos(phase_x) * scale, -np.sin(phase_x) * scale], 0)
    lines = lax.all_to_all(density, "gx", split_axis=1, concat_axis=0, tiled=True)
    result = jnp.einsum("kx,xyz->kyz", jnp.asarray(table_x, jnp.float32), lines, precision=lax.Precision.HIGH)
    spectrum = result.reshape(2, KX, lines.shape[1], lines.shape[2])
    spectrum = lax.all_to_all(
        lax.all_to_all(spectrum, "gx", split_axis=1, concat_axis=2, tiled=True),
        "gy",
        split_axis=1,
        concat_axis=2,
        tiled=True,
    )
    phase_y = phases(NY, NY, NY)
    cosine, sine = np.cos(phase_y), np.sin(phase_y)
    table_y = jnp.asarray(np.stack([np.stack([cosine, sine]), np.stack([-sine, cosine])]), jnp.float32)
    waves = jnp.einsum("cdqr,dkrz->ckqz", table_y, spectrum, precision=lax.Precision.HIGH)
    mode_rows = waves.shape[1]
    stacked = waves.reshape(2, mode_rows, MBLK, NY // MBLK, NZ)
    coupled = jnp.einsum("ckbjw,bzw->ckbjz", stacked, coupling)
    return coupled.reshape(2, mode_rows, NY, NZ)


def solution(mesh):
    return jax.shard_map(
        per_device,
        mesh=mesh,
        in_specs=(
            P(None, ("gx", "gy")),
            P(None, ("gx", "gy")),
            P(None, ("gx", "gy")),
            P(("gx", "gy")),
            P(("gx", "gy")),
            P(),
        ),
        out_specs=P(None, ("gx", "gy"), None, None),
        check_vma=False,
    )
```

time: 1330 us -> 548 us (0.41)
  matrix products: 508 us -> 32.5 us
  other arithmetic: 229 us -> 4.72 us
  blocking collectives: 283 us -> 381 us
  local copies, waits for them, and re-layouts: 150 us -> 57.4 us
  waiting for transfers between devices: 91.9 us -> 14.2 us
  Pallas kernels: 0 us -> 49.2 us
  loops' own time: 42.3 us -> 0 us
    dot_general x52 -> x3, matrix products: 508 us -> 32.5 us  [the longest x1 17.8 us: per_device(): jnp.einsum('cdqr,dkrz->ckqz', table_y, spectrum, precision=lax.Precision....]
    dynamic_update_slice x64 -> x0, other arithmetic: 205 us -> none  [spread_turn(): lax.dynamic_update_slice(extended, current + pieces[member], (plane_start...]
    all_to_all x0 -> x1, blocking collectives: none -> 97.4 us  [per_device(): lax.all_to_all(density, 'gx', split_axis=1, concat_axis=0, tiled=True)]
    all_to_all x1 -> x0, waiting for transfers between devices: 91.9 us -> none  [per_device(): lax.all_to_all(density, 'gx', split_axis=1, concat_axis=0, tiled=True)]
    dynamic_slice x80 -> x0, local copies, waits for them, and re-layouts: 66.9 us -> none  [the longest x32 50.7 us: spread_turn(): plane_part = lax.dynamic_slice_in_dim(planes, first_block, per_turn, 3)]
    pallas_call x0 -> x1, Pallas kernels: none -> 49.2 us  [spread(): pl.pallas_call(spread_kernel, out_shape=jax.ShapeDtypeStruct((cells_x + 3...]
    another operation x1 -> x0, loops' own time: 42.3 us -> none  [per_device(): lax.fori_loop(0, block_count // per_turn, spread_turn, jnp.zeros((cells_x...]
    ppermute x2, waiting for transfers between devices: 0.01 us -> 14.2 us  [from_behind(): lax.ppermute(value, axis, [(i, (i + by) % devices) for i in range(devices)])]
  transfers between devices with their start and end apart: 3 -> 2, of which waited for: 1 -> 2; matrix products, arithmetic and copies ran while one was open for 2% -> 0% of each run, Pallas kernels for 0% -> 0%
where the time goes in v1:
time: 548 us; the launch traced here: 542 us
  blocking collectives  381 us (70%)
  local copies, waits for them, and re-layouts  57.4 us (10%)
  Pallas kernels  49.2 us (9%)
  matrix products  32.5 us (6%)
  waiting for transfers between devices  14.2 us (3%)
    all_to_all x1, blocking collectives, per_device(): lax.all_to_all(lax.all_to_all(spectrum, 'gx', split_axis=1, concat_axis=2...  187 us
    all_to_all x1, blocking collectives, per_device(): lax.all_to_all(density, 'gx', split_axis=1, concat_axis=0, tiled=True)  97.4 us
    all_to_all x1, blocking collectives, per_device(): lax.all_to_all(spectrum, 'gx', split_axis=1, concat_axis=2, tiled=True)  96.6 us
    pallas_call x1, Pallas kernels, spread(): pl.pallas_call(spread_kernel, out_shape=jax.ShapeDtypeStruct((cells_x + 3...  49.2 us
    all_to_all x2, local copies, waits for them, and re-layouts, per_device(): lax.all_to_all(lax.all_to_all(spectrum, 'gx', split_axis=1, concat_axis=2...  20.2 us
    dot_general x1, matrix products, per_device(): jnp.einsum('cdqr,dkrz->ckqz', table_y, spectrum, precision=lax.Precision....  17.8 us
    ppermute x2, waiting for transfers between devices, from_behind(): lax.ppermute(value, axis, [(i, (i + by) % devices) for i in range(devices)])  14.2 us
    dot_general x1, matrix products, per_device(): jnp.einsum('kx,xyz->kyz', jnp.asarray(table_x, jnp.float32), lines, preci...  11.2 us
  transfers between devices with their start and end apart: 2, of which 2 were waited for; matrix products, arithmetic and copies ran while one was open for 0% of the time, Pallas kernels for 0%

profile of v1, /device:TPU:0, one launch (start us, length us, event | category | flops | bytes accessed | tf_op | source)
XLA Modules:
  0.0 542.2 jit_solution(2132862678679441803)
XLA Ops:
  0.0 1.1 copy.62
  2.0 1.1 copy.50
  4.5 49.2 %shard_map.82 = f32[67,136,256]{2,1,0:T(8,128)} custom-call(s32[64]{0:T(128)S(1)} %copy-done.1, s32[64]{0:T(128)S(1)} %copy-done.2, f32[10,64,128]{2,1,0:T(8,128)S(1)} %slice.52.moment_ref, f32[3,64,128]{2,1,0:T(8,128)S(1)} %bitcast.54, s32[3,64,128]{2,1,0:T(8,128)S(1)} %bitcast.55), custom_call_target="tpu_custom_call" | custom-call | tf_op jit(solution)/shard_map/pallas_call | solution.py:156
  53.7 1.0 slice.47
  55.3 1.1 slice.49
  56.3 7.5 %collective-permute-done = f32[3,131,256]{2,1,0:T(8,128)S(1)} collective-permute-done((f32[3,131,256]{2,1,0:T(8,128)S(1)}, f32[3,131,256]{2,1,0:T(8,128)S(1)}, u32[]{:S(2)}, u32[]{:S(2)}) %collective-permute-start) | collective-permute-done | bytes 402464 | tf_op jit(solution)/shard_map/ppermute | solution.py:25
  64.6 2.3 collective-permute-start.1
  67.0 6.7 %collective-permute-done.1 = f32[64,3,256]{2,1,0:T(4,128)S(1)} collective-permute-done((f32[64,3,256]{2,1,0:T(4,128)S(1)}, f32[64,3,256]{2,1,0:T(4,128)S(1)}, u32[]{:S(2)}, u32[]{:S(2)}) %collective-permute-start.1) | collective-permute-done | bytes 196640 | tf_op jit(solution)/shard_map/ppermute | solution.py:25
  73.7 4.0 fusion
  77.6 4.9 copy.33
  82.5 97.4 %all_to_all.54 = f32[64,128,256]{2,0,1:T(8,128)} all-to-all(f32[64,128,256]{2,0,1:T(8,128)S(1)} %copy.33), channel_id=1, replica_groups=mesh['gx'=8,'gy'=4] {'gx'}, dimensions={1} | all-to-all | bytes 16777216 | tf_op jit(solution)/shard_map/all_to_all | solution.py:200
  180.0 8.3 %copy.34 = f32[64,128,256]{2,1,0:T(8,128)S(1)} copy(f32[64,128,256]{2,0,1:T(8,128)} %all_to_all.54) | data formatting | bytes 16777216 | tf_op jit(solution)/shard_map/all_to_all | solution.py:200
  188.3 11.2 %fusion.5 = f32[512,16,256]{2,0,1:T(8,128)S(1)} fusion(f32[512,512,1]{1,0,2:T(8,128)S(1)} %copy-done.3, f32[512,16,256]{2,1,0:T(8,128)S(1)} %bitcast.56), kind=kOutput, calls=%fused_computation.6 | convolution fusion | flops 6442450944 | bytes 17825792 | tf_op jit(solution)/shard_map/kx,xyz->kyz/dot_general | solution.py:201
  199.5 4.9 copy.36
  204.4 96.6 %all_to_all.55 = f32[2,256,16,256]{3,2,0,1:T(8,128)S(1)} all-to-all(f32[2,256,16,256]{3,2,0,1:T(8,128)S(1)} %copy.36), channel_id=1, replica_groups=mesh['gx'=8,'gy'=4] {'gx'}, dimensions={1} | all-to-all | bytes 16777216 | tf_op jit(solution)/shard_map/all_to_all | solution.py:204
  301.0 1.4 copy.38
  302.4 1.0 copy.39
  303.4 186.7 %all_to_all.56 = f32[2,32,128,256]{3,2,0,1:T(8,128)} all-to-all(f32[2,32,128,256]{3,2,0,1:T(8,128)S(1)} %copy.39), channel_id=1, replica_groups=mesh['gx'=8,'gy'=4] {'gy'}, dimensions={1} | all-to-all | bytes 16777216 | tf_op jit(solution)/shard_map/all_to_all | solution.py:203
  490.1 9.9 %copy.41 = f32[2,8,4,128,256]{3,2,4,0,1:T(4,128)} copy(f32[2,8,4,128,256]{4,3,0,1,2:T(8,128)} %bitcast.60) | data formatting | bytes 16777216 | tf_op jit(solution)/shard_map/all_to_all | solution.py:203
  500.0 10.3 %reshape.61 = f32[2,8,512,256,1]{2,3,0,1,4:T(8,128)} reshape(f32[2,8,4,128,256]{3,2,4,0,1:T(4,128)} %copy.41) | data formatting | bytes 16777216 | tf_op jit(solution)/shard_map/all_to_all | solution.py:203
  510.3 17.8 %fusion.10 = bf16[2,8,512,256]{2,3,0,1:T(8,128)(2,1)} fusion(f32[2,2,512,512,1]{3,2,1,0,4:T(8,128)} %constant.44, f32[2,8,512,256,1]{2,3,0,1,4:T(8,128)} %reshape.61), kind=kOutput, calls=%fused_computation.9 | convolution fusion | flops 12884901888 | bytes 16777216 | tf_op jit(solution)/shard_map/cdqr,dkrz->ckqz/dot_general | solution.py:213
  528.1 6.2 %copy.42 = bf16[2,8,512,256]{3,2,1,0:T(8,128)(2,1)} copy(bf16[2,8,512,256]{2,3,0,1:T(8,128)(2,1)} %fusion.10) | data formatting | bytes 8388608 | tf_op jit(solution)/shard_map/cdqr,dkrz->ckqz/transpose | solution.py:213
  534.3 3.5 fusion.7
  537.8 4.0 copy.44
  (13 shorter events, 3.5 us)
Async XLA Ops:
  0.0 534.3 %copy-start = (f32[8,256,256]{2,1,0:T(8,128)S(1)}, f32[8,256,256]{2,1,0:T(8,128)}, u32[]{:S(2)}) copy-start(f32[8,256,256]{2,1,0:T(8,128)} %param.15) | copy-start | bytes 6291460
  3.2 0.7 copy-start.1
  3.8 0.7 copy-start.2
  54.8 9.1 %collective-permute-start = (f32[3,131,256]{2,1,0:T(8,128)S(1)}, f32[3,131,256]{2,1,0:T(8,128)S(1)}, u32[]{:S(2)}, u32[]{:S(2)}) collective-permute-start(f32[3,131,256]{2,1,0:T(8,128)S(1)} %slice.47), channel_id=1, source_target_pairs={{0,4},{4,8},{8,12},{12,16},{16,20},{20,24},{24,28},{28,0},{1,5},{5... | collective-permute-start | bytes 1207304 | tf_op jit(solution)/shard_map/ppermute | solution.py:25
  64.6 9.0 %collective-permute-start.1 = (f32[64,3,256]{2,1,0:T(4,128)S(1)}, f32[64,3,256]{2,1,0:T(4,128)S(1)}, u32[]{:S(2)}, u32[]{:S(2)}) collective-permute-start(f32[64,3,256]{2,1,0:T(4,128)S(1)} %fusion.14), channel_id=1, source_target_pairs={{0,1},{1,2},{2,3},{3,0},{4,5},{5,6},{6,7},{7,4},{8,9},{9,10},{10,1... | collective-permute-start | bytes 589832 | tf_op jit(solution)/shard_map/ppermute | solution.py:25
  180.0 8.3 %copy-start.3 = (f32[512,512,1]{1,0,2:T(8,128)S(1)}, f32[512,512,1]{1,0,2:T(8,128)}, u32[]{:S(2)}) copy-start(f32[512,512,1]{1,0,2:T(8,128)} %constant.43) | copy-start | bytes 3145732

commit v2 on v1

--- a/solution.py
+++ b/solution.py
@@ -180,6 +180,173 @@
     return (np.arange(waves)[:, None] * np.arange(cells)[None, :] % size) * (2.0 * math.pi / size)
 
 
+def exchange_kernel(
+    n_gx,
+    n_gy,
+    chunks_y,
+    grid_ref,
+    high_ref,
+    low_ref,
+    out_ref,
+    lines_ref,
+    waves_ref,
+    send_x,
+    recv_x,
+    send_k,
+    recv_k,
+    own_x,
+    own_k,
+):
+    gx = lax.axis_index("gx")
+    gy = lax.axis_index("gy")
+    devices = n_gx * n_gy
+    tall, cells_x = lines_ref.shape[0], grid_ref.shape[1]
+    height = tall // chunks_y
+    padded = waves_ref.shape[2]
+    tile = padded // chunks_y
+    modes = KX // devices
+    chunks = [(i, j) for j in range(2) for i in range(chunks_y)]
+    f32, bf16 = jnp.float32, jnp.bfloat16
+
+    def coords(r):
+        return lax.rem(gx + r // n_gy, n_gx), lax.rem(gy + lax.rem(r, n_gy), n_gy)
+
+    barrier = pltpu.get_barrier_semaphore()
+
+    def greet(r, carry):
+        tx, ty = coords(r)
+        pl.semaphore_signal(
+            barrier, inc=1, device_id=(tx, ty), device_id_type=pl.DeviceIdType.MESH
+        )
+        return carry
+
+    lax.fori_loop(1, devices, greet, 0)
+    pl.semaphore_wait(barrier, devices - 1)
+
+    def line_refs(n, tx):
+        i, j = chunks[n]
+        lanes = pl.ds(j * 128, 128)
+        source = grid_ref.at[pl.ds(tx * tall + i * height, height), :, lanes]
+        target = lines_ref.at[
+            pl.ds(i * height, height), pl.ds(pl.multiple_of(gx * cells_x, cells_x), cells_x), lanes
+        ]
+        return source, target
+
+    def line_copy(n, r):
+        tx = lax.rem(gx + r, n_gx)
+        source, target = line_refs(n, tx)
+        return pltpu.make_async_remote_copy(
+            src_ref=source,
+            dst_ref=target,
+            send_sem=send_x.at[n, r],
+            recv_sem=recv_x.at[n, r],
+            device_id=(tx, gy),
+            device_id_type=pl.DeviceIdType.MESH,
+        )
+
+    def wave_refs(n, rank):
+        i, j = chunks[n]
+        lanes = pl.ds(j * 128, 128)
+        span = pl.ds(i * tile, tile)
+        source = waves_ref.at[:, pl.ds(rank * modes, modes), span, lanes]
+        target = out_ref.at[:, :, gy * n_gx + gx, span, lanes]
+        return source, target
+
+    def wave_copy(n, r):
+        tx, ty = coords(r)
+        source, target = wave_refs(n, tx * n_gy + ty)
+        return pltpu.make_async_remote_copy(
+            src_ref=source,
+            dst_ref=target,
+            send_sem=send_k.at[n, r],
+            recv_sem=recv_k.at[n, r],
+            device_id=(tx, ty),
+            device_id_type=pl.DeviceIdType.MESH,
+        )
+
+    def own_line(n):
+        source, target = line_refs(n, gx)
+        return pltpu.make_async_copy(source, target, own_x.at[n])
+
+    def own_wave(n):
+        source, target = wave_refs(n, gx * n_gy + gy)
+        return pltpu.make_async_copy(source, target, own_k.at[n])
+
+    def each(first, last, act):
+        def body(r, carry):
+            act(r)
+            return carry
+
+        lax.fori_loop(first, last, body, 0)
+
+    for n in range(len(chunks)):
+        each(1, n_gx, lambda r: line_copy(n, r).start())
+        own_line(n).start()
+    for n, (i, j) in enumerate(chunks):
+        each(1, n_gx, lambda r: line_copy(n, r).wait_recv())
+        own_line(n).wait()
+        lanes = pl.ds(j * 128, 128)
+        for first in range(i * height, (i + 1) * height, 2):
+            picked = [y for y in (first, first + 1) if y < (i + 1) * height]
+            block = jnp.concatenate([lines_ref[y, :, lanes] for y in picked], axis=1)
+            top = block.astype(bf16)
+            rest = (block - top.astype(f32)).astype(bf16)
+            high = high_ref[...]
+            value = jnp.dot(high, top, preferred_element_type=f32)
+            value += jnp.dot(high, rest, preferred_element_type=f32)
+            value += jnp.dot(low_ref[...], top, preferred_element_type=f32)
+            for index, y in enumerate(picked):
+                row = y if tall % 8 == 0 else y - i * height
+                part = value[:, index * 128 : (index + 1) * 128]
+                waves_ref[0, :, row, lanes] = part[:KX]
+                waves_ref[1, :, row, lanes] = part[KX:]
+        each(1, devices, lambda r: wave_copy(n, r).start())
+        own_wave(n).start()
+    for n in range(len(chunks)):
+        each(1, n_gx, lambda r: line_copy(n, r).wait_send())
+        each(1, devices, lambda r: wave_copy(n, r).wait_recv())
+        each(1, devices, lambda r: wave_copy(n, r).wait_send())
+        own_wave(n).wait()
+
+
+def exchange(grid):
+    n_gx, n_gy = lax.axis_size("gx"), lax.axis_size("gy")
+    devices = n_gx * n_gy
+    cells_y, cells_x, _ = grid.shape
+    tall = cells_y // n_gx
+    chunks_y = tall // 8 if tall % 8 == 0 else 1
+    padded = -(-tall // 8) * 8
+    modes = KX // devices
+    phase_x = phases(KX, NX, NX)
+    scale = 1.0 / math.sqrt(NX * NY)
+    table = np.concatenate([np.cos(phase_x) * scale, -np.sin(phase_x) * scale], 0)
+    high = table.astype(jnp.bfloat16)
+    low = (table - high.astype(np.float64)).astype(jnp.bfloat16)
+    count = 2 * chunks_y
+    dma = pltpu.SemaphoreType.DMA
+    vmem = pl.BlockSpec(memory_space=pltpu.VMEM)
+    out = pl.pallas_call(
+        functools.partial(exchange_kernel, n_gx, n_gy, chunks_y),
+        out_shape=jax.ShapeDtypeStruct((2, modes, devices, padded, NZ), jnp.float32),
+        in_specs=[pl.BlockSpec(memory_space=pl.ANY), vmem, vmem],
+        out_specs=pl.BlockSpec(memory_space=pl.ANY),
+        scratch_shapes=[
+            pltpu.VMEM((tall, NX, NZ), jnp.float32),
+            pltpu.VMEM((2, KX, padded, NZ), jnp.float32),
+            dma((count, n_gx)),
+            dma((count, n_gx)),
+            dma((count, devices)),
+            dma((count, devices)),
+            dma((count,)),
+            dma((count,)),
+        ],
+        compiler_params=pltpu.CompilerParams(
+            collective_id=0, has_side_effects=True, vmem_limit_bytes=48 * 1024 * 1024
+        ),
+    )(grid, jnp.asarray(high), jnp.asarray(low))
+    return out[:, :, :, :tall].reshape(2, modes, NY, NZ)
+
+
 def per_device(multipoles, fractions, base_index, block_plane, atom_count, coupling):
     cells_x = NX // lax.axis_size("gx")
     cells_y = NY // lax.axis_size("gy")
@@ -194,19 +361,7 @@
         + jnp.pad(rim_x[:, :cells_y], ((0, cells_x - 3), (0, 0), (0, 0)))
         + jnp.pad(rim_y, ((0, 0), (0, cells_y - 3), (0, 0)))
     )
-    phase_x = phases(KX, NX, NX)
-    scale = 1.0 / math.sqrt(NX * NY)
-    table_x = np.concatenate([np.cos(phase_x) * scale, -np.sin(phase_x) * scale], 0)
-    lines = lax.all_to_all(density, "gx", split_axis=1, concat_axis=0, tiled=True)
-    result = jnp.einsum("kx,xyz->kyz", jnp.asarray(table_x, jnp.float32), lines, precision=lax.Precision.HIGH)
-    spectrum = result.reshape(2, KX, lines.shape[1], lines.shape[2])
-    spectrum = lax.all_to_all(
-        lax.all_to_all(spectrum, "gx", split_axis=1, concat_axis=2, tiled=True),
-        "gy",
-        split_axis=1,
-        concat_axis=2,
-        tiled=True,
-    )
+    spectrum = exchange(density.transpose(1, 0, 2))
     phase_y = phases(NY, NY, NY)
     cosine, sine = np.cos(phase_y), np.sin(phase_y)
     table_y = jnp.asarray(np.stack([np.stack([cosine, sine]), np.stack([-sine, cosine])]), jnp.float32)

time: 548 us -> 336 us (0.61)
  blocking collectives: 381 us -> 0 us
  Pallas kernels: 49.2 us -> 261 us
  local copies, waits for them, and re-layouts: 57.4 us -> 22 us
  waiting for transfers between devices: 14.2 us -> 8.14 us
    all_to_all x3 -> x0, blocking collectives: 381 us -> none  [the longest x1 187 us: per_device(): lax.all_to_all(lax.all_to_all(spectrum, 'gx', split_axis=1, concat_axis=2...]
    pallas_call x0 -> x1, Pallas kernels: none -> 212 us  [exchange(): pl.pallas_call(functools.partial(exchange_kernel, n_gx, n_gy, chunks_y),...]
    all_to_all x5 -> x0, local copies, waits for them, and re-layouts: 30.9 us -> none  [the longest x2 20.2 us: per_device(): lax.all_to_all(lax.all_to_all(spectrum, 'gx', split_axis=1, concat_axis=2...]
    dot_general x1, matrix products: 17.8 us -> 30.4 us  [per_device(): jnp.einsum('cdqr,dkrz->ckqz', table_y, spectrum, precision=lax.Precision....]
    dot_general x1 -> x0, matrix products: 11.2 us -> none  [per_device(): jnp.einsum('kx,xyz->kyz', jnp.asarray(table_x, jnp.float32), lines, preci...]
    transpose x0 -> x1, other arithmetic: none -> 6.9 us  [per_device(): spectrum = exchange(density.transpose(1, 0, 2))]
    ppermute x2, waiting for transfers between devices: 14.2 us -> 8.14 us  [from_behind(): lax.ppermute(value, axis, [(i, (i + by) % devices) for i in range(devices)])]
  transfers between devices with their start and end apart: 2 -> 2, of which waited for: 2 -> 2; matrix products, arithmetic and copies ran while one was open for 0% -> 2% of each run, Pallas kernels for 0% -> 0%
where the time goes in v2:
time: 336 us; the launch traced here: 335 us
  Pallas kernels  261 us (78%)
  matrix products  33.9 us (10%)
  local copies, waits for them, and re-layouts  22 us (7%)
  waiting for transfers between devices  8.14 us (2%)
  other arithmetic  6.91 us (2%)
    pallas_call x1, Pallas kernels, exchange(): pl.pallas_call(functools.partial(exchange_kernel, n_gx, n_gy, chunks_y),...  212 us
    pallas_call x1, Pallas kernels, spread(): pl.pallas_call(spread_kernel, out_shape=jax.ShapeDtypeStruct((cells_x + 3...  49.2 us
    dot_general x1, matrix products, per_device(): jnp.einsum('cdqr,dkrz->ckqz', table_y, spectrum, precision=lax.Precision....  30.4 us
    ppermute x2, waiting for transfers between devices, from_behind(): lax.ppermute(value, axis, [(i, (i + by) % devices) for i in range(devices)])  8.14 us
    transpose x1, other arithmetic, per_device(): spectrum = exchange(density.transpose(1, 0, 2))  6.9 us
  transfers between devices with their start and end apart: 2, of which 2 were waited for; matrix products, arithmetic and copies ran while one was open for 2% of the time, Pallas kernels for 0%

profile of v2, /device:TPU:0, one launch (start us, length us, event | category | flops | bytes accessed | tf_op | source)
XLA Modules:
  0.0 335.1 jit_solution(17666366892011452557)
XLA Ops:
  0.0 1.1 copy.64
  1.1 0.9 copy.63
  2.0 1.1 copy.43
  3.2 0.6 copy-done.3
  3.8 0.7 copy-done.4
  4.5 49.2 %shard_map.91 = f32[67,136,256]{2,1,0:T(8,128)} custom-call(s32[64]{0:T(128)S(1)} %copy-done.3, s32[64]{0:T(128)S(1)} %copy-done.4, f32[10,64,128]{2,1,0:T(8,128)S(1)} %slice.52.moment_ref, f32[3,64,128]{2,1,0:T(8,128)S(1)} %bitcast.41, s32[3,64,128]{2,1,0:T(8,128)S(1)} %bitcast.42), custom_call_target="tpu_custom_call" | custom-call | tf_op jit(solution)/shard_map/pallas_call | solution.py:156
  53.7 1.0 slice.47
  54.7 0.5 collective-permute-start
  55.2 0.7 slice.50
  56.0 1.1 slice.49
  57.1 6.7 %collective-permute-done = f32[3,131,256]{2,1,0:T(8,128)S(1)} collective-permute-done((f32[3,131,256]{2,1,0:T(8,128)S(1)}, f32[3,131,256]{2,1,0:T(8,128)S(1)}, u32[]{:S(2)}, u32[]{:S(2)}) %collective-permute-start) | collective-permute-done | bytes 402464 | tf_op jit(solution)/shard_map/ppermute | solution.py:25
  63.9 0.2 scatter-add.4
  64.1 2.4 collective-permute-start.1
  66.4 3.9 %slice.46 = f32[64,128,256]{2,1,0:T(8,128)S(1)} slice(f32[67,136,256]{2,1,0:T(8,128)} %shard_map.91), slice={[0:64], [0:128], [0:256]} | slice | bytes 16777216 | tf_op jit(solution)/shard_map/slice | solution.py:360
  70.4 0.3 copy.39
  70.7 0.0 copy-start.1
  70.7 0.0 copy-start.2
  70.7 1.4 collective-permute-done.1
  72.1 6.9 %fusion.1.grid_ref = f32[128,64,256]{2,1,0:T(8,128)} fusion(f32[64,128,256]{2,1,0:T(8,128)S(1)} %slice.46, f32[64,3,256]{2,0,1:T(8,128)S(1)} %collective-permute-done.1, f32[3,128,256]{2,0,1:T(4,128)S(1)} %copy.39), kind=kLoop, calls=%fused_computation.2 | loop fusion | flops 4194304 | bytes 17367040 | tf_op jit(solution)/shard_map/transpose | solution.py:364
  79.0 212.0 %shard_map.92 = f32[2,8,32,16,256]{4,3,2,1,0:T(8,128)} custom-call(f32[128,64,256]{2,1,0:T(8,128)} %fusion.1.grid_ref, bf16[512,512]{1,0:T(8,128)(2,1)S(1)} %copy-done.2, bf16[512,512]{1,0:T(8,128)(2,1)S(1)} %copy-done.1), custom_call_target="tpu_custom_call" | custom-call | tf_op jit(solution)/shard_map/pallas_call | solution.py:328
  291.0 30.4 %fusion.9 = bf16[2,8,512,256]{2,3,0,1:T(8,128)(2,1)} fusion(f32[2,2,512,512,1]{3,2,1,0,4:T(8,128)S(1)} %copy-done.5, f32[2,8,512,256,1]{3,2,1,0,4:T(8,128)} %bitcast.44), kind=kOutput, calls=%fused_computation.8 | convolution fusion | flops 12884901888 | bytes 16777216 | tf_op jit(solution)/shard_map/cdqr,dkrz->ckqz/dot_general | solution.py:368
  321.4 6.2 %copy.30 = bf16[2,8,512,256]{3,2,1,0:T(8,128)(2,1)} copy(bf16[2,8,512,256]{2,3,0,1:T(8,128)(2,1)} %fusion.9) | data formatting | bytes 8388608 | tf_op jit(solution)/shard_map/cdqr,dkrz->ckqz/transpose | solution.py:368
  327.6 3.5 %fusion.6 = f32[2,8,8,64,256]{4,3,1,0,2:T(8,128)S(1)} fusion(bf16[2,8,8,64,256]{4,3,2,1,0:T(8,128)(2,1)} %bitcast.43, f32[8,256,256]{2,1,0:T(8,128)S(1)} %copy-done), kind=kOutput, calls=%fused_computation.7 | convolution fusion | flops 1073741824 | bytes 14680064 | tf_op jit(solution)/shard_map/ckbjw,bzw->ckbjz/dot_general | solution.py:371
  331.1 4.0 %copy.32 = f32[2,8,8,64,256]{4,3,2,1,0:T(8,128)} copy(f32[2,8,8,64,256]{4,3,1,0,2:T(8,128)S(1)} %fusion.6) | data formatting | bytes 16777216 | tf_op jit(solution)/shard_map/ckbjw,bzw->ckbjz/transpose | solution.py:371
  (13 shorter events, 0.1 us)
Async XLA Ops:
  0.0 327.6 %copy-start = (f32[8,256,256]{2,1,0:T(8,128)S(1)}, f32[8,256,256]{2,1,0:T(8,128)}, u32[]{:S(2)}) copy-start(f32[8,256,256]{2,1,0:T(8,128)} %param.16) | copy-start | bytes 6291460
  3.2 0.7 copy-start.3
  3.8 0.7 copy-start.4
  54.7 9.1 %collective-permute-start = (f32[3,131,256]{2,1,0:T(8,128)S(1)}, f32[3,131,256]{2,1,0:T(8,128)S(1)}, u32[]{:S(2)}, u32[]{:S(2)}) collective-permute-start(f32[3,131,256]{2,1,0:T(8,128)S(1)} %slice.47), channel_id=1, source_target_pairs={{0,4},{4,8},{8,12},{12,16},{16,20},{20,24},{24,28},{28,0},{1,5},{5... | collective-permute-start | bytes 1207304 | tf_op jit(solution)/shard_map/ppermute | solution.py:25
  64.1 8.1 %collective-permute-start.1 = (f32[64,3,256]{2,0,1:T(8,128)S(1)}, f32[64,3,256]{2,0,1:T(8,128)S(1)}, u32[]{:S(2)}, u32[]{:S(2)}) collective-permute-start(f32[64,3,256]{2,0,1:T(8,128)S(1)} %scatter-add.4), channel_id=1, source_target_pairs={{0,1},{1,2},{2,3},{3,0},{4,5},{5,6},{6,7},{7,4},{8,9},{9,10},{10,1... | collective-permute-start | bytes 589832 | tf_op jit(solution)/shard_map/ppermute | solution.py:25
  70.7 8.3 %copy-start.1 = (bf16[512,512]{1,0:T(8,128)(2,1)S(1)}, bf16[512,512]{1,0:T(8,128)(2,1)}, u32[]{:S(2)}) copy-start(bf16[512,512]{1,0:T(8,128)(2,1)} %constant.37.clone.low_ref) | copy-start | bytes 1572868
  70.7 8.3 %copy-start.2 = (bf16[512,512]{1,0:T(8,128)(2,1)S(1)}, bf16[512,512]{1,0:T(8,128)(2,1)}, u32[]{:S(2)}) copy-start(bf16[512,512]{1,0:T(8,128)(2,1)} %constant.36.clone.high_ref) | copy-start | bytes 1572868
  79.0 212.0 %copy-start.5 = (f32[2,2,512,512,1]{3,2,1,0,4:T(8,128)S(1)}, f32[2,2,512,512,1]{3,2,1,0,4:T(8,128)}, u32[]{:S(2)}) copy-start(f32[2,2,512,512,1]{3,2,1,0,4:T(8,128)} %constant.43) | copy-start | bytes 12582916

commit v3 on v2

--- a/solution.py
+++ b/solution.py
@@ -347,6 +347,73 @@
     return out[:, :, :, :tall].reshape(2, modes, NY, NZ)
 
 
+def finish_kernel(table_ref, wave_ref, coupling_ref, out_ref):
+    f32, bf16 = jnp.float32, jnp.bfloat16
+    count = wave_ref.shape[1]
+    rows = NY // MBLK
+    data = [
+        jnp.concatenate([wave_ref[0, i], wave_ref[1, i]], axis=0).astype(bf16)
+        for i in range(count)
+    ]
+    data = jnp.concatenate(data, axis=1)
+
+    def one_block(b, carry):
+        start = pl.multiple_of(b * rows, rows)
+        parts = []
+        for c in range(2):
+            table = table_ref[c, pl.ds(start, rows), :]
+            value = jnp.dot(table, data, preferred_element_type=f32)
+            parts += [value[:, i * NZ : (i + 1) * NZ] for i in range(count)]
+        value = jnp.concatenate(parts, axis=0)
+        matrix = coupling_ref[b]
+        value_high = value.astype(bf16)
+        value_low = (value - value_high.astype(f32)).astype(bf16)
+        matrix_high = matrix.astype(bf16)
+        matrix_low = (matrix - matrix_high.astype(f32)).astype(bf16)
+
+        def mix(left, right):
+            return lax.dot_general(
+                left, right, (((1,), (1,)), ((), ())), preferred_element_type=f32
+            )
+
+        result = (
+            mix(value_high, matrix_high)
+            + mix(value_low, matrix_high)
+            + mix(value_high, matrix_low)
+        )
+        for c in range(2):
+            for i in range(count):
+                first = (c * count + i) * rows
+                out_ref[c, i, pl.ds(start, rows), :] = result[first : first + rows]
+        return carry
+
+    for b in range(MBLK):
+        one_block(b, 0)
+
+
+def finish(spectrum, coupling):
+    modes = spectrum.shape[1]
+    count = 2 if modes % 2 == 0 else 1
+    phase_y = phases(NY, NY, NY)
+    cosine, sine = np.cos(phase_y), np.sin(phase_y)
+    table = np.stack(
+        [np.concatenate([cosine, sine], 1), np.concatenate([-sine, cosine], 1)]
+    ).astype(jnp.bfloat16)
+    block = pl.BlockSpec((2, count, NY, NZ), lambda i: (0, i, 0, 0))
+    return pl.pallas_call(
+        finish_kernel,
+        out_shape=jax.ShapeDtypeStruct((2, modes, NY, NZ), jnp.float32),
+        grid=(modes // count,),
+        in_specs=[
+            pl.BlockSpec((2, NY, 2 * NY), lambda i: (0, 0, 0)),
+            block,
+            pl.BlockSpec((MBLK, NZ, NZ), lambda i: (0, 0, 0)),
+        ],
+        out_specs=block,
+        compiler_params=pltpu.CompilerParams(vmem_limit_bytes=40 * 1024 * 1024),
+    )(jnp.asarray(table), spectrum, coupling)
+
+
 def per_device(multipoles, fractions, base_index, block_plane, atom_count, coupling):
     cells_x = NX // lax.axis_size("gx")
     cells_y = NY // lax.axis_size("gy")
@@ -362,14 +429,7 @@
         + jnp.pad(rim_y, ((0, 0), (0, cells_y - 3), (0, 0)))
     )
     spectrum = exchange(density.transpose(1, 0, 2))
-    phase_y = phases(NY, NY, NY)
-    cosine, sine = np.cos(phase_y), np.sin(phase_y)
-    table_y = jnp.asarray(np.stack([np.stack([cosine, sine]), np.stack([-sine, cosine])]), jnp.float32)
-    waves = jnp.einsum("cdqr,dkrz->ckqz", table_y, spectrum, precision=lax.Precision.HIGH)
-    mode_rows = waves.shape[1]
-    stacked = waves.reshape(2, mode_rows, MBLK, NY // MBLK, NZ)
-    coupled = jnp.einsum("ckbjw,bzw->ckbjz", stacked, coupling)
-    return coupled.reshape(2, mode_rows, NY, NZ)
+    return finish(spectrum, coupling)
 
 
 def solution(mesh):

time: 336 us -> 315 us (0.938)
  matrix products: 33.9 us -> 0 us
  Pallas kernels: 261 us -> 281 us
  local copies, waits for them, and re-layouts: 22 us -> 15 us
    dot_general x2 -> x0, matrix products: 33.9 us -> none  [the longest x1 30.4 us: per_device(): jnp.einsum('cdqr,dkrz->ckqz', table_y, spectrum, precision=lax.Precision....]
    pallas_call x0 -> x1, Pallas kernels: none -> 20.4 us  [finish(): pl.pallas_call(finish_kernel, out_shape=jax.ShapeDtypeStruct((2, modes, N...]
    transpose x2 -> x0, local copies, waits for them, and re-layouts: 10.2 us -> none  [the longest x1 6.18 us: per_device(): jnp.einsum('cdqr,dkrz->ckqz', table_y, spectrum, precision=lax.Precision....]
    unnamed x17 -> x19, local copies, waits for them, and re-layouts: 4.75 us -> 7.98 us
where the time goes in v3:
time: 315 us; the launch traced here: 314 us
  Pallas kernels  281 us (89%)
  local copies, waits for them, and re-layouts  15 us (5%)
  waiting for transfers between devices  8.14 us (3%)
  other arithmetic  6.91 us (2%)
    pallas_call x1, Pallas kernels, exchange(): pl.pallas_call(functools.partial(exchange_kernel, n_gx, n_gy, chunks_y),...  212 us
    pallas_call x1, Pallas kernels, spread(): pl.pallas_call(spread_kernel, out_shape=jax.ShapeDtypeStruct((cells_x + 3...  49.2 us
    pallas_call x1, Pallas kernels, finish(): pl.pallas_call(finish_kernel, out_shape=jax.ShapeDtypeStruct((2, modes, N...  20.4 us
    ppermute x2, waiting for transfers between devices, from_behind(): lax.ppermute(value, axis, [(i, (i + by) % devices) for i in range(devices)])  8.14 us
    unnamed x19, local copies, waits for them, and re-layouts  7.98 us
    transpose x1, other arithmetic, per_device(): spectrum = exchange(density.transpose(1, 0, 2))  6.9 us
  transfers between devices with their start and end apart: 2, of which 2 were waited for; matrix products, arithmetic and copies ran while one was open for 2% of the time, Pallas kernels for 0%

profile of v3, /device:TPU:0, one launch (start us, length us, event | category | flops | bytes accessed | tf_op | source)
XLA Modules:
  0.0 314.4 jit_solution(6748255471966075109)
XLA Ops:
  0.0 0.9 copy.37
  0.9 0.9 copy.36
  1.8 1.1 copy.24
  3.0 0.0 copy-start.5
  3.0 0.6 copy-done.5
  3.7 0.7 copy-done.6
  4.3 49.2 %shard_map.91 = f32[67,136,256]{2,1,0:T(8,128)} custom-call(s32[64]{0:T(128)S(1)} %copy-done.5, s32[64]{0:T(128)S(1)} %copy-done.6, f32[10,64,128]{2,1,0:T(8,128)S(1)} %slice.52.moment_ref, f32[3,64,128]{2,1,0:T(8,128)S(1)} %bitcast.15, s32[3,64,128]{2,1,0:T(8,128)S(1)} %bitcast.16), custom_call_target="tpu_custom_call" | custom-call | tf_op jit(solution)/shard_map/pallas_call | solution.py:156
  53.5 1.0 slice.47
  54.6 0.5 collective-permute-start
  55.1 0.7 slice.50
  55.8 1.1 slice.49
  57.0 6.7 %collective-permute-done = f32[3,131,256]{2,1,0:T(8,128)S(1)} collective-permute-done((f32[3,131,256]{2,1,0:T(8,128)S(1)}, f32[3,131,256]{2,1,0:T(8,128)S(1)}, u32[]{:S(2)}, u32[]{:S(2)}) %collective-permute-start) | collective-permute-done | bytes 402464 | tf_op jit(solution)/shard_map/ppermute | solution.py:25
  63.7 0.2 scatter-add.4
  63.9 2.4 collective-permute-start.1
  66.3 3.9 %slice.46 = f32[64,128,256]{2,1,0:T(8,128)S(1)} slice(f32[67,136,256]{2,1,0:T(8,128)} %shard_map.91), slice={[0:64], [0:128], [0:256]} | slice | bytes 16777216 | tf_op jit(solution)/shard_map/slice | solution.py:427
  70.3 0.3 copy.20
  70.5 0.0 copy-start.3
  70.6 0.0 copy-start.4
  70.6 1.4 collective-permute-done.1
  72.0 6.9 %fusion.1.grid_ref = f32[128,64,256]{2,1,0:T(8,128)} fusion(f32[64,128,256]{2,1,0:T(8,128)S(1)} %slice.46, f32[64,3,256]{2,0,1:T(8,128)S(1)} %collective-permute-done.1, f32[3,128,256]{2,0,1:T(4,128)S(1)} %copy.20), kind=kLoop, calls=%fused_computation.2 | loop fusion | flops 4194304 | bytes 17367040 | tf_op jit(solution)/shard_map/transpose | solution.py:431
  78.9 0.0 copy-done.3
  78.9 211.7 %shard_map.92 = f32[2,8,32,16,256]{4,3,2,1,0:T(8,128)} custom-call(f32[128,64,256]{2,1,0:T(8,128)} %fusion.1.grid_ref, bf16[512,512]{1,0:T(8,128)(2,1)S(1)} %copy-done.4, bf16[512,512]{1,0:T(8,128)(2,1)S(1)} %copy-done.3), custom_call_target="tpu_custom_call" | custom-call | tf_op jit(solution)/shard_map/pallas_call | solution.py:328
  290.6 3.4 %copy-done = f32[2,8,32,16,256]{4,3,2,1,0:T(8,128)S(1)} copy-done((f32[2,8,32,16,256]{4,3,2,1,0:T(8,128)S(1)}, f32[2,8,32,16,256]{4,3,2,1,0:T(8,128)}, u32[]{:S(2)}) %copy-start) | copy-done | bytes 8388632
  294.0 20.4 %shard_map.93 = f32[2,8,512,256]{3,2,1,0:T(8,128)} custom-call(bf16[2,512,1024]{2,1,0:T(8,128)(2,1)S(1)} %copy-done.2, f32[2,8,512,256]{3,2,1,0:T(8,128)S(1)} %bitcast.14, f32[8,256,256]{2,1,0:T(8,128)S(1)} %copy-done.1), custom_call_target="tpu_custom_call" | custom-call | tf_op jit(solution)/shard_map/pallas_call | solution.py:403
  (12 shorter events, 0.1 us)
Async XLA Ops:
  3.0 0.7 copy-start.5
  3.7 0.7 copy-start.6
  54.6 9.1 %collective-permute-start = (f32[3,131,256]{2,1,0:T(8,128)S(1)}, f32[3,131,256]{2,1,0:T(8,128)S(1)}, u32[]{:S(2)}, u32[]{:S(2)}) collective-permute-start(f32[3,131,256]{2,1,0:T(8,128)S(1)} %slice.47), channel_id=1, source_target_pairs={{0,4},{4,8},{8,12},{12,16},{16,20},{20,24},{24,28},{28,0},{1,5},{5... | collective-permute-start | bytes 1207304 | tf_op jit(solution)/shard_map/ppermute | solution.py:25
  63.9 8.1 %collective-permute-start.1 = (f32[64,3,256]{2,0,1:T(8,128)S(1)}, f32[64,3,256]{2,0,1:T(8,128)S(1)}, u32[]{:S(2)}, u32[]{:S(2)}) collective-permute-start(f32[64,3,256]{2,0,1:T(8,128)S(1)} %scatter-add.4), channel_id=1, source_target_pairs={{0,1},{1,2},{2,3},{3,0},{4,5},{5,6},{6,7},{7,4},{8,9},{9,10},{10,1... | collective-permute-start | bytes 589832 | tf_op jit(solution)/shard_map/ppermute | solution.py:25
  70.5 8.3 %copy-start.3 = (bf16[512,512]{1,0:T(8,128)(2,1)S(1)}, bf16[512,512]{1,0:T(8,128)(2,1)}, u32[]{:S(2)}) copy-start(bf16[512,512]{1,0:T(8,128)(2,1)} %constant.37.clone.low_ref) | copy-start | bytes 1572868
  70.6 8.3 %copy-start.4 = (bf16[512,512]{1,0:T(8,128)(2,1)S(1)}, bf16[512,512]{1,0:T(8,128)(2,1)}, u32[]{:S(2)}) copy-start(bf16[512,512]{1,0:T(8,128)(2,1)} %constant.36.clone.high_ref) | copy-start | bytes 1572868
  78.9 211.7 %copy-start.1 = (f32[8,256,256]{2,1,0:T(8,128)S(1)}, f32[8,256,256]{2,1,0:T(8,128)}, u32[]{:S(2)}) copy-start(f32[8,256,256]{2,1,0:T(8,128)} %coupling_ref.1) | copy-start | bytes 6291460
  78.9 211.7 %copy-start.2 = (bf16[2,512,1024]{2,1,0:T(8,128)(2,1)S(1)}, bf16[2,512,1024]{2,1,0:T(8,128)(2,1)}, u32[]{:S(2)}) copy-start(bf16[2,512,1024]{2,1,0:T(8,128)(2,1)} %constant.38.clone.table_ref) | copy-start | bytes 6291460
  290.6 3.4 %copy-start = (f32[2,8,32,16,256]{4,3,2,1,0:T(8,128)S(1)}, f32[2,8,32,16,256]{4,3,2,1,0:T(8,128)}, u32[]{:S(2)}) copy-start(f32[2,8,32,16,256]{4,3,2,1,0:T(8,128)} %shard_map.92) | copy-start | bytes 25165828

commit v4 on v3

--- a/solution.py
+++ b/solution.py
@@ -286,6 +286,7 @@
         each(1, n_gx, lambda r: line_copy(n, r).wait_recv())
         own_line(n).wait()
         lanes = pl.ds(j * 128, 128)
+        columns = []
         for first in range(i * height, (i + 1) * height, 2):
             picked = [y for y in (first, first + 1) if y < (i + 1) * height]
             block = jnp.concatenate([lines_ref[y, :, lanes] for y in picked], axis=1)
@@ -295,11 +296,11 @@
             value = jnp.dot(high, top, preferred_element_type=f32)
             value += jnp.dot(high, rest, preferred_element_type=f32)
             value += jnp.dot(low_ref[...], top, preferred_element_type=f32)
-            for index, y in enumerate(picked):
-                row = y if tall % 8 == 0 else y - i * height
-                part = value[:, index * 128 : (index + 1) * 128]
-                waves_ref[0, :, row, lanes] = part[:KX]
-                waves_ref[1, :, row, lanes] = part[KX:]
+            columns += [value[:, m * 128 : (m + 1) * 128] for m in range(len(picked))]
+        columns += [jnp.zeros_like(columns[0])] * (tile - height)
+        turned = jnp.swapaxes(jnp.stack(columns, axis=0), 0, 1)
+        waves_ref[0, :, i * tile : (i + 1) * tile, lanes] = turned[:KX]
+        waves_ref[1, :, i * tile : (i + 1) * tile, lanes] = turned[KX:]
         each(1, devices, lambda r: wave_copy(n, r).start())
         own_wave(n).start()
     for n in range(len(chunks)):
@@ -347,7 +348,7 @@
     return out[:, :, :, :tall].reshape(2, modes, NY, NZ)
 
 
-def finish_kernel(table_ref, wave_ref, coupling_ref, out_ref):
+def finish_kernel(table_ref, wave_ref, coupling_ref, out_ref, rows_ref):
     f32, bf16 = jnp.float32, jnp.bfloat16
     count = wave_ref.shape[1]
     rows = NY // MBLK
@@ -356,13 +357,14 @@
         for i in range(count)
     ]
     data = jnp.concatenate(data, axis=1)
+    for c in range(2):
+        rows_ref[c] = jnp.dot(table_ref[c], data, preferred_element_type=f32)
 
     def one_block(b, carry):
-        start = pl.multiple_of(b * rows, rows)
+        start = b * rows
         parts = []
         for c in range(2):
-            table = table_ref[c, pl.ds(start, rows), :]
-            value = jnp.dot(table, data, preferred_element_type=f32)
+            value = rows_ref[c, pl.ds(start, rows), :]
             parts += [value[:, i * NZ : (i + 1) * NZ] for i in range(count)]
         value = jnp.concatenate(parts, axis=0)
         matrix = coupling_ref[b]
@@ -410,6 +412,7 @@
             pl.BlockSpec((MBLK, NZ, NZ), lambda i: (0, 0, 0)),
         ],
         out_specs=block,
+        scratch_shapes=[pltpu.VMEM((2, NY, count * NZ), jnp.float32)],
         compiler_params=pltpu.CompilerParams(vmem_limit_bytes=40 * 1024 * 1024),
     )(jnp.asarray(table), spectrum, coupling)
 

time: 315 us -> 304 us (0.965)
  Pallas kernels: 281 us -> 270 us
    pallas_call x1, Pallas kernels: 20.4 us -> 10.3 us  [finish(): pl.pallas_call(finish_kernel, out_shape=jax.ShapeDtypeStruct((2, modes, N...]
where the time goes in v4:
time: 304 us; the launch traced here: 303 us
  Pallas kernels  270 us (89%)
  local copies, waits for them, and re-layouts  15 us (5%)
  waiting for transfers between devices  8.14 us (3%)
  other arithmetic  6.91 us (2%)
    pallas_call x1, Pallas kernels, exchange(): pl.pallas_call(functools.partial(exchange_kernel, n_gx, n_gy, chunks_y),...  211 us
    pallas_call x1, Pallas kernels, spread(): pl.pallas_call(spread_kernel, out_shape=jax.ShapeDtypeStruct((cells_x + 3...  49.2 us
    pallas_call x1, Pallas kernels, finish(): pl.pallas_call(finish_kernel, out_shape=jax.ShapeDtypeStruct((2, modes, N...  10.3 us
    ppermute x2, waiting for transfers between devices, from_behind(): lax.ppermute(value, axis, [(i, (i + by) % devices) for i in range(devices)])  8.14 us
    unnamed x19, local copies, waits for them, and re-layouts  7.98 us
    transpose x1, other arithmetic, per_device(): spectrum = exchange(density.transpose(1, 0, 2))  6.9 us
  transfers between devices with their start and end apart: 2, of which 2 were waited for; matrix products, arithmetic and copies ran while one was open for 2% of the time, Pallas kernels for 0%

profile of v4, /device:TPU:0, one launch (start us, length us, event | category | flops | bytes accessed | tf_op | source)
XLA Modules:
  0.0 303.3 jit_solution(17848401086053196990)
XLA Ops:
  0.0 0.9 copy.37
  0.9 0.9 copy.36
  1.8 1.1 copy.24
  3.0 0.0 copy-start.5
  3.0 0.6 copy-done.5
  3.7 0.7 copy-done.6
  4.3 49.2 %shard_map.91 = f32[67,136,256]{2,1,0:T(8,128)} custom-call(s32[64]{0:T(128)S(1)} %copy-done.5, s32[64]{0:T(128)S(1)} %copy-done.6, f32[10,64,128]{2,1,0:T(8,128)S(1)} %slice.52.moment_ref, f32[3,64,128]{2,1,0:T(8,128)S(1)} %bitcast.15, s32[3,64,128]{2,1,0:T(8,128)S(1)} %bitcast.16), custom_call_target="tpu_custom_call" | custom-call | tf_op jit(solution)/shard_map/pallas_call | solution.py:156
  53.5 1.0 slice.47
  54.6 0.5 collective-permute-start
  55.1 0.7 slice.50
  55.8 1.1 slice.49
  57.0 6.7 %collective-permute-done = f32[3,131,256]{2,1,0:T(8,128)S(1)} collective-permute-done((f32[3,131,256]{2,1,0:T(8,128)S(1)}, f32[3,131,256]{2,1,0:T(8,128)S(1)}, u32[]{:S(2)}, u32[]{:S(2)}) %collective-permute-start) | collective-permute-done | bytes 402464 | tf_op jit(solution)/shard_map/ppermute | solution.py:25
  63.7 0.2 scatter-add.4
  63.9 2.4 collective-permute-start.1
  66.3 3.9 %slice.46 = f32[64,128,256]{2,1,0:T(8,128)S(1)} slice(f32[67,136,256]{2,1,0:T(8,128)} %shard_map.91), slice={[0:64], [0:128], [0:256]} | slice | bytes 16777216 | tf_op jit(solution)/shard_map/slice | solution.py:430
  70.3 0.3 copy.20
  70.5 0.0 copy-start.3
  70.6 0.0 copy-start.4
  70.6 1.4 collective-permute-done.1
  72.0 6.9 %fusion.1.grid_ref = f32[128,64,256]{2,1,0:T(8,128)} fusion(f32[64,128,256]{2,1,0:T(8,128)S(1)} %slice.46, f32[64,3,256]{2,0,1:T(8,128)S(1)} %collective-permute-done.1, f32[3,128,256]{2,0,1:T(4,128)S(1)} %copy.20), kind=kLoop, calls=%fused_computation.2 | loop fusion | flops 4194304 | bytes 17367040 | tf_op jit(solution)/shard_map/transpose | solution.py:434
  78.9 0.0 copy-done.3
  78.9 210.7 %shard_map.92 = f32[2,8,32,16,256]{4,3,2,1,0:T(8,128)} custom-call(f32[128,64,256]{2,1,0:T(8,128)} %fusion.1.grid_ref, bf16[512,512]{1,0:T(8,128)(2,1)S(1)} %copy-done.4, bf16[512,512]{1,0:T(8,128)(2,1)S(1)} %copy-done.3), custom_call_target="tpu_custom_call" | custom-call | tf_op jit(solution)/shard_map/pallas_call | solution.py:329
  289.6 3.4 %copy-done = f32[2,8,32,16,256]{4,3,2,1,0:T(8,128)S(1)} copy-done((f32[2,8,32,16,256]{4,3,2,1,0:T(8,128)S(1)}, f32[2,8,32,16,256]{4,3,2,1,0:T(8,128)}, u32[]{:S(2)}) %copy-start) | copy-done | bytes 8388632
  293.0 10.3 %shard_map.93 = f32[2,8,512,256]{3,2,1,0:T(8,128)} custom-call(bf16[2,512,1024]{2,1,0:T(8,128)(2,1)S(1)} %copy-done.2, f32[2,8,512,256]{3,2,1,0:T(8,128)S(1)} %bitcast.14, f32[8,256,256]{2,1,0:T(8,128)S(1)} %copy-done.1), custom_call_target="tpu_custom_call" | custom-call | tf_op jit(solution)/shard_map/pallas_call | solution.py:405
  (12 shorter events, 0.1 us)
Async XLA Ops:
  3.0 0.7 copy-start.5
  3.7 0.7 copy-start.6
  54.6 9.1 %collective-permute-start = (f32[3,131,256]{2,1,0:T(8,128)S(1)}, f32[3,131,256]{2,1,0:T(8,128)S(1)}, u32[]{:S(2)}, u32[]{:S(2)}) collective-permute-start(f32[3,131,256]{2,1,0:T(8,128)S(1)} %slice.47), channel_id=1, source_target_pairs={{0,4},{4,8},{8,12},{12,16},{16,20},{20,24},{24,28},{28,0},{1,5},{5... | collective-permute-start | bytes 1207304 | tf_op jit(solution)/shard_map/ppermute | solution.py:25
  63.9 8.1 %collective-permute-start.1 = (f32[64,3,256]{2,0,1:T(8,128)S(1)}, f32[64,3,256]{2,0,1:T(8,128)S(1)}, u32[]{:S(2)}, u32[]{:S(2)}) collective-permute-start(f32[64,3,256]{2,0,1:T(8,128)S(1)} %scatter-add.4), channel_id=1, source_target_pairs={{0,1},{1,2},{2,3},{3,0},{4,5},{5,6},{6,7},{7,4},{8,9},{9,10},{10,1... | collective-permute-start | bytes 589832 | tf_op jit(solution)/shard_map/ppermute | solution.py:25
  70.5 8.3 %copy-start.3 = (bf16[512,512]{1,0:T(8,128)(2,1)S(1)}, bf16[512,512]{1,0:T(8,128)(2,1)}, u32[]{:S(2)}) copy-start(bf16[512,512]{1,0:T(8,128)(2,1)} %constant.37.clone.low_ref) | copy-start | bytes 1572868
  70.6 8.3 %copy-start.4 = (bf16[512,512]{1,0:T(8,128)(2,1)S(1)}, bf16[512,512]{1,0:T(8,128)(2,1)}, u32[]{:S(2)}) copy-start(bf16[512,512]{1,0:T(8,128)(2,1)} %constant.36.clone.high_ref) | copy-start | bytes 1572868
  78.9 210.7 %copy-start.1 = (f32[8,256,256]{2,1,0:T(8,128)S(1)}, f32[8,256,256]{2,1,0:T(8,128)}, u32[]{:S(2)}) copy-start(f32[8,256,256]{2,1,0:T(8,128)} %coupling_ref.1) | copy-start | bytes 6291460
  78.9 210.7 %copy-start.2 = (bf16[2,512,1024]{2,1,0:T(8,128)(2,1)S(1)}, bf16[2,512,1024]{2,1,0:T(8,128)(2,1)}, u32[]{:S(2)}) copy-start(bf16[2,512,1024]{2,1,0:T(8,128)(2,1)} %constant.38.clone.table_ref) | copy-start | bytes 6291460
  289.6 3.4 %copy-start = (f32[2,8,32,16,256]{4,3,2,1,0:T(8,128)S(1)}, f32[2,8,32,16,256]{4,3,2,1,0:T(8,128)}, u32[]{:S(2)}) copy-start(f32[2,8,32,16,256]{4,3,2,1,0:T(8,128)} %shard_map.92) | copy-start | bytes 25165828
